TPU v7x, 512 devices: a whole 4x4x16 slice. The times are simulated.
512 devices in a mesh: space: 32 (over x_hi, z), modes: 16 (over y, x_lo, core).
Axes of the slice: x: 4 (x_hi: 2, x_lo: 2; x = x_hi * 2 + x_lo), y: 4, z: 16, core: 2. Of those that a mesh axis runs over, the one named last changes fastest.
Arguments:
- mode_field: bfloat16 [64, 128, 256, 256], P('space', 'modes'), may hold values from -8 to 8
- diffusion: float32 [64, 256, 256], P('space'), may hold values from 0.1 to 0.16
- joule_load: float32 [64, 256, 256], P('space'), may hold values from 0.5 to 1.5
- chaos_basis: bfloat16 [343, 128], replicated, may hold values from -0.5 to 0.5
- quad_weight: float32 [343], replicated, may hold values from 0.25 to 1
- base_conductivity: float32 [343], replicated, may hold values from 0.5 to 2
- thermal_slope: float32 [343], replicated, may hold values from 0.2 to 0.8
Outputs:
- advanced: bfloat16 [64, 128, 256, 256], P('space', 'modes')
All inputs are finite; a program needn't handle non-finite values.
Results may differ from a plain program's by a relative error of at most 0.0054.
Values may be sent and summed in bfloat16 or wider, within the bound.
A program may use at most 64 MiB of HBM per device.

v0:
```python
import jax
import jax.numpy as jnp
from jax import lax
from jax.sharding import PartitionSpec as P


def with_halo(x, sides, width):
    for axis, dim in sides:
        size, length = (lax.axis_size(axis), x.shape[dim])
        up = [(i, (i + 1) % size) for i in range(size - 1)]
        down = [(j, i) for i, j in up]
        last = lax.slice_in_dim(x, length - width, length, axis=dim)
        initial = lax.slice_in_dim(x, 0, width, axis=dim)
        before = lax.ppermute(last, axis, up)
        after = lax.ppermute(initial, axis, down)
        x = jnp.concatenate([before, x, after], axis=dim)
    return x


def advance(extended, rate_mid):
    middle = extended[1:-1]
    padded_xy = jnp.pad(middle, ((0, 0), (0, 0), (1, 1), (1, 1)))
    beside = extended[2:] + extended[:-2]
    beside = beside + padded_xy[:, :, 2:, 1:-1] + padded_xy[:, :, :-2, 1:-1]
    beside = beside + padded_xy[:, :, 1:-1, 2:] + padded_xy[:, :, 1:-1, :-2]
    return middle + rate_mid[:, None] * (beside - 6.0 * middle)


def on_device(
    mode_field, diffusion, joule_load, chaos_basis, quad_weight, base_conductivity, thermal_slope
):
    extended = with_halo(mode_field, (("space", 0),), 1).astype(jnp.float32)
    first = advance(extended, diffusion)
    second_ext = with_halo(first, (("space", 0),), 1)
    values = advance(second_ext, diffusion)
    settled = values.astype(jnp.bfloat16)
    point_temp = jnp.einsum(
        "qm,zmxy->zqxy",
        chaos_basis,
        lax.all_to_all(settled, "modes", split_axis=2, concat_axis=1, tiled=True),
        preferred_element_type=jnp.float32,
    )
    conductivity = base_conductivity[:, None, None] * (
        1.0 + thermal_slope[:, None, None] * jnp.tanh(point_temp)
    )
    weighted = (quad_weight[:, None, None] * conductivity).astype(jnp.bfloat16)
    summed = jnp.einsum("qm,zqxy->zmxy", chaos_basis, weighted, preferred_element_type=jnp.float32)
    cell_source = summed.astype(jnp.bfloat16)
    projected = lax.all_to_all(cell_source, "modes", split_axis=1, concat_axis=2, tiled=True)
    kept_modes = lax.optimization_barrier(settled).astype(jnp.float32)
    return (kept_modes + joule_load[:, None] * projected.astype(jnp.float32)).astype(jnp.bfloat16)


def solution(mesh):
    return jax.shard_map(
        on_device,
        mesh=mesh,
        in_specs=(
            P("space", "modes", None, None),
            P("space", None, None),
            P("space", None, None),
            P(),
            P(),
            P(),
            P(),
        ),
        out_specs=P("space", "modes", None, None),
        check_vma=False,
    )
```

profile of v0, /device:TPU:4, one launch (start us, length us, event | category | flops | bytes accessed | tf_op | source)
XLA Modules:
  0.0 198.7 jit_solution(8916879316402831475)
XLA Ops:
  0.0 1.8 fusion.33
  1.8 3.8 %collective-permute-start = (bf16[1,8,256,256]{3,2,1,0:T(8,128)(2,1)S(1)}, bf16[1,8,256,256]{3,2,1,0:T(8,128)(2,1)S(1)}, u32[]{:S(2)}, u32[]{:S(2)}) collective-permute-start(bf16[1,8,256,256]{3,2,1,0:T(8,128)(2,1)S(1)} %get-tuple-element.7), channel_id=1, source_target_pairs={{0,16},{16,32},{32,48},{48,64},{64,80},{80,96},{96,112},{112,128},... | collective-permute-start | bytes 3145736 | tf_op jit(solution)/shard_map/ppermute | solution.py:14
  5.7 9.4 %collective-permute-start.1 = (bf16[1,8,256,256]{3,2,1,0:T(8,128)(2,1)S(1)}, bf16[1,8,256,256]{3,2,1,0:T(8,128)(2,1)S(1)}, u32[]{:S(2)}, u32[]{:S(2)}) collective-permute-start(bf16[1,8,256,256]{3,2,1,0:T(8,128)(2,1)S(1)} %get-tuple-element.8), channel_id=1, source_target_pairs={{16,0},{32,16},{48,32},{64,48},{80,64},{96,80},{112,96},{128,112},... | collective-permute-start | bytes 3145736 | tf_op jit(solution)/shard_map/ppermute | solution.py:15
  15.1 21.2 %collective-permute-done = bf16[1,8,256,256]{3,2,1,0:T(8,128)(2,1)S(1)} collective-permute-done((bf16[1,8,256,256]{3,2,1,0:T(8,128)(2,1)S(1)}, bf16[1,8,256,256]{3,2,1,0:T(8,128)(2,1)S(1)}, u32[]{:S(2)}, u32[]{:S(2)}) %collective-permute-start) | collective-permute-done | bytes 1048608 | tf_op jit(solution)/shard_map/ppermute | solution.py:14
  36.3 1.2 collective-permute-done.1
  37.5 0.7 maximum_convert_fusion
  38.2 2.3 %slice.70 = f32[2,8,256,256]{3,2,1,0:T(8,128)} slice(f32[4,8,256,256]{3,2,1,0:T(8,128)S(1)} %maximum_convert_fusion), slice={[1:3], [0:8], [0:256], [0:256]} | slice | bytes 8388608 | tf_op jit(solution)/shard_map/slice | solution.py:21
  40.5 10.5 %fusion.9 = f32[2,8,256,256]{3,2,1,0:T(8,128)S(1)} fusion(f32[2,8,256,256]{3,2,1,0:T(8,128)} %slice.70, f32[4,8,256,256]{3,2,1,0:T(8,128)S(1)} %maximum_convert_fusion, f32[2,256,256]{2,1,0:T(8,128)} %param.8), kind=kLoop, calls=%fused_computation.17 | loop fusion | flops 9437184 | bytes 17301504 | tf_op jit(solution)/shard_map/add | solution.py:26
  51.0 0.0 copy-start.4
  51.1 0.4 fusion.32
  51.5 8.0 %collective-permute-start.2 = (f32[1,8,256,256]{3,2,1,0:T(8,128)S(1)}, f32[1,8,256,256]{3,2,1,0:T(8,128)S(1)}, u32[]{:S(2)}, u32[]{:S(2)}) collective-permute-start(f32[1,8,256,256]{3,2,1,0:T(8,128)S(1)} %get-tuple-element.5), channel_id=1, source_target_pairs={{16,0},{32,16},{48,32},{64,48},{80,64},{96,80},{112,96},{128,112},... | collective-permute-start | bytes 6291464 | tf_op jit(solution)/shard_map/ppermute | solution.py:15
  59.5 1.9 collective-permute-start.3
  61.4 42.1 %collective-permute-done.2 = f32[1,8,256,256]{3,2,1,0:T(8,128)S(1)} collective-permute-done((f32[1,8,256,256]{3,2,1,0:T(8,128)S(1)}, f32[1,8,256,256]{3,2,1,0:T(8,128)S(1)}, u32[]{:S(2)}, u32[]{:S(2)}) %collective-permute-start.2) | collective-permute-done | bytes 2097184 | tf_op jit(solution)/shard_map/ppermute | solution.py:15
  103.5 7.9 %collective-permute-done.3 = f32[1,8,256,256]{3,2,1,0:T(8,128)} collective-permute-done((f32[1,8,256,256]{3,2,1,0:T(8,128)S(1)}, f32[1,8,256,256]{3,2,1,0:T(8,128)}, u32[]{:S(2)}, u32[]{:S(2)}) %collective-permute-start.3) | collective-permute-done | bytes 2097184 | tf_op jit(solution)/shard_map/ppermute | solution.py:14
  111.5 4.8 %fusion.17 = bf16[2,8,256,256]{3,2,1,0:T(8,128)(2,1)S(1)} fusion(f32[2,8,256,256]{3,2,1,0:T(8,128)S(1)} %fusion.9, f32[1,8,256,256]{3,2,1,0:T(8,128)} %collective-permute-done.3, f32[1,8,256,256]{3,2,1,0:T(8,128)S(1)} %collective-permute-done.2, f32[2,256,256]{2,1,0:T(8,128)S(1)} %copy-done.4), kind=kLoop, calls=%fused_computation.25 | loop fusion | flops 12582912 | bytes 11010048 | tf_op jit(solution)/shard_map/convert_element_type | solution.py:36
  116.2 1.2 copy.14
  117.4 0.0 copy-start.6
  117.4 0.0 copy-start.7
  117.4 0.0 copy-start.8
  117.5 33.8 %all_to_all.27 = bf16[2,8,256,256]{3,1,0,2:T(8,128)(2,1)S(1)} all-to-all(bf16[2,8,256,256]{3,1,0,2:T(8,128)(2,1)S(1)} %copy.14), channel_id=1, replica_groups=mesh['space'=32,'modes'=16] {'modes'}, dimensions={2} | all-to-all | bytes 4194304 | tf_op jit(solution)/shard_map/all_to_all | solution.py:40
  151.2 0.7 copy.16
  152.0 6.0 %convert_bitcast_fusion.1 = bf16[2,128,16,256]{1,3,2,0:T(8,128)(2,1)} fusion(f32[343]{0:T(512)S(1)} %copy-done.6, f32[343]{0:T(512)S(1)} %copy-done.7, f32[343]{0:T(512)S(1)} %copy-done.8, bf16[2,128,16,256]{3,2,1,0:T(8,128)(2,1)S(1)} %bitcast.29, bf16[343,128]{1,0:T(8,128)(2,1)S(1)} %copy-done), kind=kOutput, calls=%fused_computation.37 | convolution fusion | flops 1453744128 | bytes 4286228 | tf_op jit(solution)/shard_map/qm,zqxy->zmxy/dot_general | solution.py:47
  157.9 4.5 %copy.18 = bf16[2,128,16,256]{3,2,0,1:T(8,128)(2,1)} copy(bf16[2,128,16,256]{1,3,2,0:T(8,128)(2,1)} %convert_bitcast_fusion.1) | data formatting | bytes 4194304 | tf_op jit(solution)/shard_map/convert_element_type | solution.py:48
  162.5 3.7 %all-to-all-start.1 = ((bf16[2,128,16,256]{3,2,0,1:T(8,128)(2,1)}), bf16[2,128,16,256]{3,2,0,1:T(8,128)(2,1)S(1)}, u32[]{:S(2)}, u32[]{:S(2)}) async-start(bf16[2,128,16,256]{3,2,0,1:T(8,128)(2,1)} %copy.18), calls=%async_computation.1 | async-start | bytes 4194304 | tf_op jit(solution)/shard_map/all_to_all | solution.py:49
  166.2 27.9 %all-to-all-done.1 = bf16[2,128,16,256]{3,2,0,1:T(8,128)(2,1)S(1)} async-done(((bf16[2,128,16,256]{3,2,0,1:T(8,128)(2,1)}), bf16[2,128,16,256]{3,2,0,1:T(8,128)(2,1)S(1)}, u32[]{:S(2)}, u32[]{:S(2)}) %all-to-all-start.1) | async-done | bytes 2097184 | tf_op jit(solution)/shard_map/all_to_all | solution.py:49
  194.0 0.2 copy.19
  194.2 0.6 convert_bitcast_fusion
  194.8 0.0 copy-start.5
  194.8 0.5 copy.20
  195.3 1.1 copy-done.2
  196.4 0.1 copy-done.5
  196.5 2.2 %fusion.20 = bf16[2,8,256,256]{3,2,1,0:T(8,128)(2,1)} fusion(f32[2,8,16,16,256]{4,3,2,1,0:T(8,128)S(1)} %copy.20, bf16[2,8,256,256]{3,2,1,0:T(8,128)(2,1)S(1)} %copy-done.2, f32[2,256,256]{2,1,0:T(8,128)S(1)} %copy-done.5), kind=kLoop, calls=%fused_computation.34 | loop fusion | flops 4194304 | bytes 8912896 | tf_op jit(solution)/shard_map/convert_element_type | solution.py:51
  (11 shorter events, 0.0 us)
Async XLA Ops:
  0.0 151.9 %copy-start = (bf16[343,128]{1,0:T(8,128)(2,1)S(1)}, bf16[343,128]{1,0:T(8,128)(2,1)}, u32[]{:S(2)}) copy-start(bf16[343,128]{1,0:T(8,128)(2,1)} %param.10) | copy-start | bytes 263428
  0.0 37.5 %copy-start.3 = (bf16[2,8,256,256]{3,2,1,0:T(8,128)(2,1)S(1)}, bf16[2,8,256,256]{3,2,1,0:T(8,128)(2,1)}, u32[]{:S(2)}) copy-start(bf16[2,8,256,256]{3,2,1,0:T(8,128)(2,1)} %param.7) | copy-start | bytes 6291460
  1.8 34.5 %collective-permute-start = (bf16[1,8,256,256]{3,2,1,0:T(8,128)(2,1)S(1)}, bf16[1,8,256,256]{3,2,1,0:T(8,128)(2,1)S(1)}, u32[]{:S(2)}, u32[]{:S(2)}) collective-permute-start(bf16[1,8,256,256]{3,2,1,0:T(8,128)(2,1)S(1)} %get-tuple-element.7), channel_id=1, source_target_pairs={{0,16},{16,32},{32,48},{48,64},{64,80},{80,96},{96,112},{112,128},... | collective-permute-start | bytes 3145736 | tf_op jit(solution)/shard_map/ppermute | solution.py:14
  5.7 31.8 %collective-permute-start.1 = (bf16[1,8,256,256]{3,2,1,0:T(8,128)(2,1)S(1)}, bf16[1,8,256,256]{3,2,1,0:T(8,128)(2,1)S(1)}, u32[]{:S(2)}, u32[]{:S(2)}) collective-permute-start(bf16[1,8,256,256]{3,2,1,0:T(8,128)(2,1)S(1)} %get-tuple-element.8), channel_id=1, source_target_pairs={{16,0},{32,16},{48,32},{64,48},{80,64},{96,80},{112,96},{128,112},... | collective-permute-start | bytes 3145736 | tf_op jit(solution)/shard_map/ppermute | solution.py:15
  51.0 60.4 %copy-start.4 = (f32[2,256,256]{2,1,0:T(8,128)S(1)}, f32[2,256,256]{2,1,0:T(8,128)}, u32[]{:S(2)}) copy-start(f32[2,256,256]{2,1,0:T(8,128)} %param.8) | copy-start | bytes 1572868
  51.5 52.0 %collective-permute-start.2 = (f32[1,8,256,256]{3,2,1,0:T(8,128)S(1)}, f32[1,8,256,256]{3,2,1,0:T(8,128)S(1)}, u32[]{:S(2)}, u32[]{:S(2)}) collective-permute-start(f32[1,8,256,256]{3,2,1,0:T(8,128)S(1)} %get-tuple-element.5), channel_id=1, source_target_pairs={{16,0},{32,16},{48,32},{64,48},{80,64},{96,80},{112,96},{128,112},... | collective-permute-start | bytes 6291464 | tf_op jit(solution)/shard_map/ppermute | solution.py:15
  59.5 51.9 %collective-permute-start.3 = (f32[1,8,256,256]{3,2,1,0:T(8,128)S(1)}, f32[1,8,256,256]{3,2,1,0:T(8,128)}, u32[]{:S(2)}, u32[]{:S(2)}) collective-permute-start(f32[1,8,256,256]{3,2,1,0:T(8,128)S(1)} %get-tuple-element.6), channel_id=1, source_target_pairs={{0,16},{16,32},{32,48},{48,64},{64,80},{80,96},{96,112},{112,128},... | collective-permute-start | bytes 6291464 | tf_op jit(solution)/shard_map/ppermute | solution.py:14
  116.2 35.0 %copy-start.1 = (bf16[2,8,256,256]{3,2,1,0:T(8,128)(2,1)}, bf16[2,8,256,256]{3,2,1,0:T(8,128)(2,1)S(1)}, u32[]{:S(2)}) copy-start(bf16[2,8,256,256]{3,2,1,0:T(8,128)(2,1)S(1)} %fusion.17) | copy-start | bytes 6291460
  117.4 34.5 %copy-start.6 = (f32[343]{0:T(512)S(1)}, f32[343]{0:T(512)}, u32[]{:S(2)}) copy-start(f32[343]{0:T(512)} %param.11) | copy-start | bytes 4120
  117.4 34.5 %copy-start.7 = (f32[343]{0:T(512)S(1)}, f32[343]{0:T(512)}, u32[]{:S(2)}) copy-start(f32[343]{0:T(512)} %param.13) | copy-start | bytes 4120
  117.4 34.5 %copy-start.8 = (f32[343]{0:T(512)S(1)}, f32[343]{0:T(512)}, u32[]{:S(2)}) copy-start(f32[343]{0:T(512)} %param.12) | copy-start | bytes 4120
  162.5 31.6 %all-to-all-start.1 = ((bf16[2,128,16,256]{3,2,0,1:T(8,128)(2,1)}), bf16[2,128,16,256]{3,2,0,1:T(8,128)(2,1)S(1)}, u32[]{:S(2)}, u32[]{:S(2)}) async-start(bf16[2,128,16,256]{3,2,0,1:T(8,128)(2,1)} %copy.18), calls=%async_computation.1 | async-start | bytes 4194304 | tf_op jit(solution)/shard_map/all_to_all | solution.py:49
  194.8 1.6 copy-start.2
  194.8 1.7 copy-start.5
where the time goes:
time: 199 us
  waiting for transfers between devices  100 us (50%)
  blocking collectives  33.8 us (17%)
  starting transfers between devices  26.9 us (14%)
  other arithmetic  18.7 us (9%)
  local copies, waits for them, and re-layouts  12.9 us (6%)
  matrix products  5.96 us (3%)
    ppermute x2, waiting for transfers between devices, with_halo(): after = lax.ppermute(initial, axis, down)  43.2 us
    all_to_all x1, blocking collectives, on_device(): lax.all_to_all(settled, 'modes', split_axis=2, concat_axis=1, tiled=True)  33.8 us
    ppermute x2, waiting for transfers between devices, with_halo(): before = lax.ppermute(last, axis, up)  29.2 us
    all_to_all x1, waiting for transfers between devices, on_device(): lax.all_to_all(cell_source, 'modes', split_axis=1, concat_axis=2, tiled=T...  27.9 us
    ppermute x2, starting transfers between devices, with_halo(): after = lax.ppermute(initial, axis, down)  17.4 us
    add x1, other arithmetic, advance(): return middle + rate_mid[:, None] * (beside - 6.0 * middle)  10.5 us
    dot_general x1, matrix products, on_device(): jnp.einsum('qm,zqxy->zmxy', chaos_basis, weighted, preferred_element_type...  5.96 us
    ppermute x2, starting transfers between devices, with_halo(): before = lax.ppermute(last, axis, up)  5.75 us
  transfers between devices with their start and end apart: 5, of which 5 were waited for; matrix products, arithmetic and copies ran while one was open for 0% of the time, Pallas kernels for 0%

commit v1 on v0

v1 whole, which is shorter than its diff:
```python
import functools

import jax
import jax.numpy as jnp
from jax import lax
from jax.experimental import pallas as pl
from jax.experimental.pallas import tpu as pltpu
from jax.sharding import PartitionSpec as P

MESH = pl.DeviceIdType.MESH
F32 = jnp.float32
BF16 = jnp.bfloat16

NX = 256
NY = 256
LANES = 128
GROUPS = NX // 16
DEV = 16
SPACE = 32
CHUNKS = 4
E = NX // CHUNKS
R = E // DEV
QP = 352


def halves(row):
    return row[..., :LANES], row[..., LANES:]


def beside_y(low, high, first_lane, last_lane):
    up_l, up_h = pltpu.roll(low, 1, 1), pltpu.roll(high, 1, 1)
    dn_l, dn_h = pltpu.roll(low, LANES - 1, 1), pltpu.roll(high, LANES - 1, 1)
    sum_l = jnp.where(first_lane, 0.0, up_l) + jnp.where(last_lane, dn_h, dn_l)
    sum_h = jnp.where(first_lane, up_l, up_h) + jnp.where(last_lane, 0.0, dn_h)
    return sum_l, sum_h


def swap_planes(a):
    return jnp.concatenate([a[8:], a[:8]], axis=0)


def spread(tile0, tile1, k):
    return jnp.concatenate(
        [
            jnp.broadcast_to(tile0[k : k + 1], (8, LANES)),
            jnp.broadcast_to(tile1[k : k + 1], (8, LANES)),
        ],
        axis=0,
    )


def kernel(
    v_ref, d_ref, joule_ref, w1_ref, w2_ref, bias_ref, out_ref,
    to_l, to_r, from_l, from_r, part, first, settled, gathered, projected, returned,
    halo_send, halo_recv, fwd_send, fwd_recv, back_send, back_recv,
):
    s = lax.axis_index("space")
    m = lax.axis_index("modes")

    barrier = pltpu.get_barrier_semaphore()

    def greet(k, _):
        pl.semaphore_signal(
            barrier, inc=1, device_id=(s, lax.rem(m + k, DEV)), device_id_type=MESH
        )
        return 0

    lax.fori_loop(1, DEV, greet, 0)

    @pl.when(s > 0)
    def _():
        pl.semaphore_signal(barrier, inc=1, device_id=(s - 1, m), device_id_type=MESH)

    @pl.when(s < SPACE - 1)
    def _():
        pl.semaphore_signal(barrier, inc=1, device_id=(s + 1, m), device_id_type=MESH)

    lane = lax.broadcasted_iota(jnp.int32, (16, LANES), 1)
    first_lane, last_lane = lane == 0, lane == LANES - 1

    def row_of(ref, x):
        return halves(ref[x].astype(F32))

    def sweep_group(g, _):
        x0 = g * 16
        before = row_of(v_ref, lax.rem(x0 + NX - 1, NX))
        before = tuple(jnp.where(g == 0, 0.0, b) for b in before)
        after = row_of(v_ref, lax.rem(x0 + 16, NX))
        after = tuple(jnp.where(g == GROUPS - 1, 0.0, a) for a in after)
        rows = [before] + [row_of(v_ref, x0 + k) for k in range(16)] + [after]
        rate = [halves(d_ref[z, pl.ds(x0, 16), :]) for z in range(2)]
        for k in range(16):
            here = rows[k + 1]
            across = beside_y(*here, first_lane, last_lane)
            for h in range(2):
                mid = here[h]
                sides = rows[k][h] + rows[k + 2][h] + across[h] + swap_planes(mid)
                g_row = mid + spread(rate[0][h], rate[1][h], k) * (sides - 6.0 * mid)
                cols = pl.ds(h * LANES, LANES)
                part[x0 + k, :, cols] = g_row
                to_l[g, k, :, cols] = jnp.concatenate([mid[:8], g_row[:8]], axis=0).astype(BF16)
                to_r[g, k, :, cols] = jnp.concatenate([mid[8:], g_row[8:]], axis=0).astype(BF16)
        to_l[g, 16] = d_ref[0, pl.ds(x0, 16), :].astype(BF16)
        to_r[g, 16] = d_ref[1, pl.ds(x0, 16), :].astype(BF16)
        return 0

    def span(c):
        a = 0 if c == 0 else c * (E // 16) + 1
        b = GROUPS if c == CHUNKS - 1 else (c + 1) * (E // 16) + 1
        return a, b - a

    def halo_copies(c):
        a, n = span(c)
        left = pltpu.make_async_remote_copy(
            src_ref=to_l.at[pl.ds(a, n)],
            dst_ref=from_r.at[pl.ds(a, n)],
            send_sem=halo_send.at[0, c],
            recv_sem=halo_recv.at[0, c],
            device_id=(s - 1, m),
            device_id_type=MESH,
        )
        right = pltpu.make_async_remote_copy(
            src_ref=to_r.at[pl.ds(a, n)],
            dst_ref=from_l.at[pl.ds(a, n)],
            send_sem=halo_send.at[1, c],
            recv_sem=halo_recv.at[1, c],
            device_id=(s + 1, m),
            device_id_type=MESH,
        )
        return left, right

    @pl.when(s == 0)
    def _():
        def clear(g, _):
            from_l[g] = jnp.zeros((17, 16, NY), BF16)
            return 0

        lax.fori_loop(0, GROUPS, clear, 0)

    @pl.when(s == SPACE - 1)
    def _():
        def clear(g, _):
            from_r[g] = jnp.zeros((17, 16, NY), BF16)
            return 0

        lax.fori_loop(0, GROUPS, clear, 0)

    first[0] = jnp.zeros((16, NY), F32)
    first[NX + 1] = jnp.zeros((16, NY), F32)

    for c in range(CHUNKS):
        a, n = span(c)
        lax.fori_loop(a, a + n, sweep_group, 0)
        if c == 0:
            inner = (s > 0) & (s < SPACE - 1)

            @pl.when(inner)
            def _():
                pl.semaphore_wait(barrier, DEV + 1)

            @pl.when(jnp.logical_not(inner))
            def _():
                pl.semaphore_wait(barrier, DEV)

        left, right = halo_copies(c)
        pl.when(s > 0)(left.start)
        pl.when(s < SPACE - 1)(right.start)

    def finish_group(g, _):
        x0 = g * 16
        rate = [halves(d_ref[z, pl.ds(x0, 16), :]) for z in range(2)]
        for k in range(16):
            near_l, near_r = from_l[g, k], from_r[g, k]
            for h in range(2):
                cols = pl.ds(h * LANES, LANES)
                vl = near_l[:, h * LANES : (h + 1) * LANES].astype(F32)
                vr = near_r[:, h * LANES : (h + 1) * LANES].astype(F32)
                outer = jnp.concatenate([vl[:8], vr[:8]], axis=0)
                first[x0 + k + 1, :, cols] = (
                    part[x0 + k, :, cols] + spread(rate[0][h], rate[1][h], k) * outer
                )
        return 0

    def second_group(g, _):
        x0 = g * 16
        rate = [halves(d_ref[z, pl.ds(x0, 16), :]) for z in range(2)]
        outer_rate = [halves(ref[g, 16].astype(F32)) for ref in (from_l, from_r)]
        rows = [halves(first[x0 + k]) for k in range(18)]
        for k in range(16):
            here = rows[k + 1]
            across = beside_y(*here, first_lane, last_lane)
            v_row = row_of(v_ref, x0 + k)
            near_l, near_r = row_of(from_l.at[g], k), row_of(from_r.at[g], k)
            for h in range(2):
                mid = here[h]
                outer = jnp.concatenate([near_l[h][8:], near_r[h][8:]], axis=0)
                outer = outer + spread(outer_rate[0][h], outer_rate[1][h], k) * v_row[h]
                sides = rows[k][h] + rows[k + 2][h] + across[h] + swap_planes(mid) + outer
                value = mid + spread(rate[0][h], rate[1][h], k) * (sides - 6.0 * mid)
                settled[x0 + k, :, pl.ds(h * LANES, LANES)] = value.astype(BF16)
        return 0

    def fwd_copy(c, j, send=fwd_send, recv=fwd_recv):
        return pltpu.make_async_remote_copy(
            src_ref=settled.at[pl.ds(c * E + j * R, R)],
            dst_ref=gathered.at[c, m],
            send_sem=send.at[c],
            recv_sem=recv.at[c],
            device_id=(s, j),
            device_id_type=MESH,
        )

    def back_copy(c, j):
        return pltpu.make_async_remote_copy(
            src_ref=projected.at[c, j],
            dst_ref=returned.at[pl.ds(c * E + m * R, R)],
            send_sem=back_send.at[c],
            recv_sem=back_recv.at[c],
            device_id=(s, j),
            device_id_type=MESH,
        )

    def stage_stencil(c):
        for chunk in range(CHUNKS):

            @pl.when(c == chunk)
            def _():
                left, right = halo_copies(chunk)
                pl.when(s < SPACE - 1)(left.wait_recv)
                pl.when(s > 0)(right.wait_recv)
                a, n = span(chunk)
                lax.fori_loop(a, a + n, finish_group, 0)

        n = E // 16
        lax.fori_loop(c * n, (c + 1) * n, second_group, 0)

        def send(k, _):
            fwd_copy(c, lax.rem(m + k, DEV)).start()
            return 0

        lax.fori_loop(1, DEV, send, 0)
        pltpu.make_async_copy(
            settled.at[pl.ds(c * E + m * R, R)], gathered.at[c, m], fwd_recv.at[c]
        ).start()

    def stage_evaluate(c):
        pltpu.make_async_copy(gathered.at[c], gathered.at[c], fwd_recv.at[c]).wait()

        def one(r, _):
            cells = gathered[c, :, r].reshape(16 * DEV, NY)
            temp = jnp.dot(w1_ref[...], cells, preferred_element_type=F32)
            heat = jnp.tanh(temp).astype(BF16)
            source = jnp.dot(w2_ref[...], heat, preferred_element_type=F32)
            source = source + bias_ref[:, :1]
            projected[c, :, r] = source.astype(BF16).reshape(DEV, 16, NY)
            return 0

        lax.fori_loop(0, R, one, 0)

        def send(k, _):
            back_copy(c, lax.rem(m + k, DEV)).start()
            return 0

        lax.fori_loop(1, DEV, send, 0)
        pltpu.make_async_copy(
            projected.at[c, m], returned.at[pl.ds(c * E + m * R, R)], back_recv.at[c]
        ).start()

    def stage_finish(c):
        rows = returned.at[pl.ds(c * E, E)]
        pltpu.make_async_copy(rows, rows, back_recv.at[c]).wait()

        def group(g, _):
            x0 = g * 16
            load = [halves(joule_ref[z, pl.ds(x0, 16), :]) for z in range(2)]
            for k in range(16):
                kept, source = row_of(settled, x0 + k), row_of(returned, x0 + k)
                for h in range(2):
                    value = kept[h] + spread(load[0][h], load[1][h], k) * source[h]
                    out_ref[x0 + k, :, pl.ds(h * LANES, LANES)] = value.astype(BF16)
            return 0

        n = E // 16
        lax.fori_loop(c * n, (c + 1) * n, group, 0)

    def step(t, _):
        @pl.when(t < CHUNKS)
        def _():
            stage_stencil(t)

        @pl.when((t >= 1) & (t < CHUNKS + 1))
        def _():
            stage_evaluate(t - 1)

        @pl.when(t >= 2)
        def _():
            stage_finish(t - 2)

        return 0

    lax.fori_loop(0, CHUNKS + 2, step, 0)

    for c in range(CHUNKS):
        left, right = halo_copies(c)
        pl.when(s > 0)(left.wait_send)
        pl.when(s < SPACE - 1)(right.wait_send)
        sent = settled.at[pl.ds(0, (DEV - 1) * R)]
        pltpu.make_async_copy(sent, sent, fwd_send.at[c]).wait()
        pltpu.make_async_copy(sent, sent, back_send.at[c]).wait()


def on_device(
    mode_field, diffusion, joule_load, chaos_basis, quad_weight, base_conductivity, thermal_slope
):
    planes, modes = mode_field.shape[:2]
    points = chaos_basis.shape[0]
    field = jnp.transpose(mode_field, (2, 0, 1, 3)).reshape(NX, planes * modes, NY)

    level = quad_weight * base_conductivity
    swing = level * thermal_slope
    basis = chaos_basis.astype(F32)
    eye = jnp.eye(planes, dtype=F32)
    pad = ((0, QP - points), (0, 0))
    split = jnp.pad(basis, pad).reshape(QP, DEV, modes)
    w1 = split[None, :, :, None, :] * eye[:, None, None, :, None]
    w1 = w1.reshape(planes * QP, DEV * planes * modes).astype(BF16)
    split = jnp.pad(basis * swing[:, None], pad).reshape(QP, DEV, modes)
    split = jnp.transpose(split, (1, 2, 0))
    w2 = split[:, None, :, None, :] * eye[None, :, None, :, None]
    w2 = w2.reshape(DEV * planes * modes, planes * QP).astype(BF16)
    bias = jnp.sum(basis * level[:, None], axis=0).reshape(DEV, 1, modes, 1)
    bias = jnp.broadcast_to(bias, (DEV, planes, modes, LANES)).reshape(-1, LANES)

    vmem = pl.BlockSpec(memory_space=pltpu.VMEM)
    rows16 = (NX, 16, NY)
    halo = (GROUPS, 17, 16, NY)
    out = pl.pallas_call(
        kernel,
        out_shape=jax.ShapeDtypeStruct(rows16, BF16),
        in_specs=[vmem] * 6,
        out_specs=vmem,
        scratch_shapes=[
            pltpu.VMEM(halo, BF16),
            pltpu.VMEM(halo, BF16),
            pltpu.VMEM(halo, BF16),
            pltpu.VMEM(halo, BF16),
            pltpu.VMEM(rows16, F32),
            pltpu.VMEM((NX + 2, 16, NY), F32),
            pltpu.VMEM(rows16, BF16),
            pltpu.VMEM((CHUNKS, DEV, R, 16, NY), BF16),
            pltpu.VMEM((CHUNKS, DEV, R, 16, NY), BF16),
            pltpu.VMEM(rows16, BF16),
            pltpu.SemaphoreType.DMA((2, CHUNKS)),
            pltpu.SemaphoreType.DMA((2, CHUNKS)),
            pltpu.SemaphoreType.DMA((CHUNKS,)),
            pltpu.SemaphoreType.DMA((CHUNKS,)),
            pltpu.SemaphoreType.DMA((CHUNKS,)),
            pltpu.SemaphoreType.DMA((CHUNKS,)),
        ],
        compiler_params=pltpu.CompilerParams(
            collective_id=0, has_side_effects=True, vmem_limit_bytes=56 * 2**20
        ),
        cost_estimate=pl.CostEstimate(
            flops=3 * 10**9, bytes_accessed=6 * 2**20, transcendentals=3 * 10**6
        ),
    )(field, diffusion, joule_load, w1, w2, bias)
    return jnp.transpose(out.reshape(NX, planes, modes, NY), (1, 2, 0, 3))


def solution(mesh):
    return jax.shard_map(
        on_device,
        mesh=mesh,
        in_specs=(
            P("space", "modes", None, None),
            P("space", None, None),
            P("space", None, None),
            P(),
            P(),
            P(),
            P(),
        ),
        out_specs=P("space", "modes", None, None),
        check_vma=False,
    )
```

time: 199 us -> 127 us (0.64)
  the two profiles are of different devices: /device:TPU:4 before, /device:TPU:1 now
where the time goes in v1:
time: 127 us
  Pallas kernels  115 us (91%)
  local copies, waits for them, and re-layouts  10.5 us (8%)
  other arithmetic  1.49 us (1%)
    pallas_call x1, Pallas kernels, on_device(): pl.pallas_call(kernel, out_shape=jax.ShapeDtypeStruct(rows16, BF16), in_s...  115 us
    reshape x1, local copies, waits for them, and re-layouts, on_device(): return jnp.transpose(out.reshape(NX, planes, modes, NY), (1, 2, 0, 3))  3.63 us

profile of v1, /device:TPU:1, one launch (start us, length us, event | category | flops | bytes accessed | tf_op | source)
XLA Modules:
  0.0 126.6 jit_solution(15558148045750128931)
XLA Ops:
  0.0 0.1 copy.13
  0.1 0.7 fusion
  0.8 1.0 copy.12
  1.8 0.1 multiply_reduce_fusion
  1.9 0.1 broadcast_in_dim.16
  2.1 0.1 broadcast_in_dim.18
  2.2 0.0 copy-start
  2.2 0.7 broadcast_in_dim.19.bias_ref
  3.0 0.3 multiply_convert_fusion.1
  3.3 0.3 convert_element_type.32
  3.6 0.9 copy.14.w1_ref
  4.5 0.3 multiply_convert_fusion
  4.8 1.1 convert_element_type.34.w2_ref
  5.9 0.0 copy-done
  5.9 2.5 %copy.19 = bf16[256,2,8,256]{3,2,1,0:T(8,128)(2,1)} copy(bf16[256,2,8,256]{3,0,2,1:T(8,128)(2,1)S(1)} %bitcast.16) | data formatting | bytes 4194304 | tf_op jit(solution)/shard_map/transpose | solution.py:317
  8.4 114.6 %shard_map.73 = bf16[256,16,256]{2,1,0:T(8,128)(2,1)} custom-call(bf16[256,16,256]{2,1,0:T(8,128)(2,1)} %bitcast.18, f32[2,256,256]{2,1,0:T(8,128)} %d_ref.1, f32[2,256,256]{2,1,0:T(8,128)} %joule_ref.1, bf16[704,256]{1,0:T(8,128)(2,1)} %copy.14.w1_ref, bf16[256,704]{1,0:T(8,128)(2,1)} %convert_element_type.34.w2_ref, f32[256,128]{1,0:T(8,128)} %broadcast_in_dim.19.bias_ref), custom_call_target="tpu_custom_call" | custom-call | flops 3000000000 | bytes 6291456 | tf_op jit(solution)/shard_map/pallas_call | solution.py:337
  123.0 3.6 %copy.18 = bf16[256,2,8,256]{3,0,2,1:T(8,128)(2,1)} copy(bf16[256,2,8,256]{3,2,1,0:T(8,128)(2,1)} %bitcast.17) | data formatting | bytes 4194304 | tf_op jit(solution)/shard_map/reshape | solution.py:367
  (5 shorter events, 0.1 us)
Async XLA Ops:
  2.2 3.7 %copy-start = (bf16[2,8,256,256]{3,2,1,0:T(8,128)(2,1)S(1)}, bf16[2,8,256,256]{3,2,1,0:T(8,128)(2,1)}, u32[]{:S(2)}) copy-start(bf16[2,8,256,256]{3,2,1,0:T(8,128)(2,1)} %param.7) | copy-start | bytes 6291460

commit v2 on v1

--- a/solution.py
+++ b/solution.py
@@ -17,7 +17,8 @@
 GROUPS = NX // 16
 DEV = 16
 SPACE = 32
-CHUNKS = 4
+FAR = SPACE // 2
+CHUNKS = 8
 E = NX // CHUNKS
 R = E // DEV
 QP = 352
@@ -50,9 +51,11 @@
 
 
 def kernel(
-    v_ref, d_ref, joule_ref, w1_ref, w2_ref, bias_ref, out_ref,
-    to_l, to_r, from_l, from_r, part, first, settled, gathered, projected, returned,
-    halo_send, halo_recv, fwd_send, fwd_recv, back_send, back_recv,
+    field_ref, d_ref, joule_ref, basis_ref, weight_ref, base_ref, slope_ref, out_ref,
+    v_ref, swap,
+    to_l, to_r, from_l, from_r, relayed, part, first, settled, gathered, projected, returned,
+    w1, w2, bias,
+    halo_send, halo_recv, relay_recv, fwd_send, fwd_recv, back_send, back_recv,
 ):
     s = lax.axis_index("space")
     m = lax.axis_index("modes")
@@ -75,14 +78,39 @@
     def _():
         pl.semaphore_signal(barrier, inc=1, device_id=(s + 1, m), device_id_type=MESH)
 
+    is_end = (s == 0) | (s == SPACE - 1)
+    is_far = (s == FAR - 1) | (s == FAR)
+    by_relay = (lax.rem(m, 2) == 1) & (is_end | is_far)
+    across = lax.rem(s + FAR, SPACE)
+    around = lax.rem(s // FAR * 2 * FAR + FAR + SPACE - 1 - s, SPACE)
+
+    @pl.when(by_relay)
+    def _():
+        pl.semaphore_signal(barrier, inc=1, device_id=(across, m), device_id_type=MESH)
+        pl.semaphore_signal(barrier, inc=1, device_id=(around, m), device_id_type=MESH)
+
     lane = lax.broadcasted_iota(jnp.int32, (16, LANES), 1)
     first_lane, last_lane = lane == 0, lane == LANES - 1
 
     def row_of(ref, x):
         return halves(ref[x].astype(F32))
 
+    to_row = lax.broadcasted_iota(jnp.int32, (256, 256), 0)
+    from_row = lax.broadcasted_iota(jnp.int32, (256, 256), 1)
+    swapped = (to_row // 16 == from_row % 16) & (to_row % 16 == from_row // 16)
+    swap[...] = jnp.where(swapped, 1.0, 0.0).astype(BF16)
+
+    def regroup(g):
+        x0 = g * 16
+        block = field_ref[:, :, pl.ds(x0, 16), :].reshape(256, NY)
+        rows = jnp.dot(swap[...], block, preferred_element_type=F32)
+        v_ref[pl.ds(x0, 16)] = rows.astype(BF16).reshape(16, 16, NY)
+
+    regroup(0)
+
     def sweep_group(g, _):
         x0 = g * 16
+        regroup(lax.rem(g + 1, GROUPS))
         before = row_of(v_ref, lax.rem(x0 + NX - 1, NX))
         before = tuple(jnp.where(g == 0, 0.0, b) for b in before)
         after = row_of(v_ref, lax.rem(x0 + 16, NX))
@@ -109,8 +137,77 @@
         b = GROUPS if c == CHUNKS - 1 else (c + 1) * (E // 16) + 1
         return a, b - a
 
+    def relay_copy(c, source, side):
+        a, n = span(c)
+        return pltpu.make_async_remote_copy(
+            src_ref=source.at[pl.ds(a, n)],
+            dst_ref=relayed.at[pl.ds(a, n)],
+            send_sem=halo_send.at[side, c],
+            recv_sem=relay_recv.at[c],
+            device_id=(across, m),
+            device_id_type=MESH,
+        )
+
+    def forward_copy(c, target, side):
+        a, n = span(c)
+        return pltpu.make_async_remote_copy(
+            src_ref=relayed.at[pl.ds(a, n)],
+            dst_ref=target.at[pl.ds(a, n)],
+            send_sem=halo_send.at[side, c],
+            recv_sem=halo_recv.at[side, c],
+            device_id=(around, m),
+            device_id_type=MESH,
+        )
+
+    def forward(c):
+        if span(c)[1] == 0:
+            return
+
+        @pl.when(by_relay & (s == 0))
+        def _():
+            copy = forward_copy(c, from_r, 0)
+            relay_copy(c, to_l, 0).wait_recv()
+            copy.start()
+
+        @pl.when(by_relay & (s == SPACE - 1))
+        def _():
+            copy = forward_copy(c, from_l, 1)
+            relay_copy(c, to_r, 1).wait_recv()
+            copy.start()
+
+    def prepare():
+        count = basis_ref.shape[0]
+        basis = jnp.concatenate(
+            [basis_ref[...].astype(F32), jnp.zeros((QP - count, LANES), F32)], axis=0
+        ).astype(BF16)
+        fill = jnp.zeros((1, QP - count), F32)
+
+        def twice(row):
+            return jnp.concatenate([row, fill, row, fill], axis=1)
+
+        modes = lax.broadcasted_iota(jnp.int32, (DEV * 8, DEV * 16), 0)
+        place = lax.broadcasted_iota(jnp.int32, (DEV * 8, DEV * 16), 1)
+        base = place // 16 * 8 + place % 8
+        level = (weight_ref[...] * base_ref[...])[None]
+        swing = twice(level * slope_ref[...][None])
+        level = twice(level)
+        zero = jnp.zeros_like(basis)
+        spread_out = 0.0
+        for z in range(2):
+            pick = jnp.where((modes == base) & (place % 16 // 8 == z), 1.0, 0.0).astype(BF16)
+            w1[z * QP : (z + 1) * QP] = jnp.dot(basis, pick, preferred_element_type=F32).astype(BF16)
+            rows = jnp.concatenate([basis, zero] if z == 0 else [zero, basis], axis=0)
+            spread_out = spread_out + lax.dot_general(
+                pick, rows, (((0,), (1,)), ((), ())), preferred_element_type=F32
+            )
+        w2[...] = (spread_out * swing).astype(BF16)
+        total = jnp.sum(spread_out * level, axis=1, keepdims=True)
+        bias[...] = jnp.broadcast_to(total, (DEV * 16, LANES))
+
     def halo_copies(c):
         a, n = span(c)
+        if n == 0:
+            return None, None
         left = pltpu.make_async_remote_copy(
             src_ref=to_l.at[pl.ds(a, n)],
             dst_ref=from_r.at[pl.ds(a, n)],
@@ -152,19 +249,20 @@
         a, n = span(c)
         lax.fori_loop(a, a + n, sweep_group, 0)
         if c == 0:
-            inner = (s > 0) & (s < SPACE - 1)
-
-            @pl.when(inner)
-            def _():
-                pl.semaphore_wait(barrier, DEV + 1)
-
-            @pl.when(jnp.logical_not(inner))
-            def _():
-                pl.semaphore_wait(barrier, DEV)
+            ends = jnp.where(is_end, 1, 0)
+            pl.semaphore_wait(barrier, DEV + 1 - ends + jnp.where(by_relay, 2, 0))
 
         left, right = halo_copies(c)
-        pl.when(s > 0)(left.start)
-        pl.when(s < SPACE - 1)(right.start)
+        if left is None:
+            continue
+        relay = by_relay & is_far
+        pl.when((s > 0) & jnp.logical_not(relay & (s == FAR)))(left.start)
+        pl.when((s < SPACE - 1) & jnp.logical_not(relay & (s == FAR - 1)))(right.start)
+        pl.when(relay & (s == FAR))(relay_copy(c, to_l, 0).start)
+        pl.when(relay & (s == FAR - 1))(relay_copy(c, to_r, 1).start)
+
+    forward(0)
+    prepare()
 
     def finish_group(g, _):
         x0 = g * 16
@@ -225,11 +323,14 @@
 
             @pl.when(c == chunk)
             def _():
+                if chunk < CHUNKS - 1:
+                    forward(chunk + 1)
                 left, right = halo_copies(chunk)
-                pl.when(s < SPACE - 1)(left.wait_recv)
-                pl.when(s > 0)(right.wait_recv)
-                a, n = span(chunk)
-                lax.fori_loop(a, a + n, finish_group, 0)
+                if left is not None:
+                    pl.when(s < SPACE - 1)(left.wait_recv)
+                    pl.when(s > 0)(right.wait_recv)
+                    a, n = span(chunk)
+                    lax.fori_loop(a, a + n, finish_group, 0)
 
         n = E // 16
         lax.fori_loop(c * n, (c + 1) * n, second_group, 0)
@@ -248,10 +349,10 @@
 
         def one(r, _):
             cells = gathered[c, :, r].reshape(16 * DEV, NY)
-            temp = jnp.dot(w1_ref[...], cells, preferred_element_type=F32)
+            temp = jnp.dot(w1[...], cells, preferred_element_type=F32)
             heat = jnp.tanh(temp).astype(BF16)
-            source = jnp.dot(w2_ref[...], heat, preferred_element_type=F32)
-            source = source + bias_ref[:, :1]
+            source = jnp.dot(w2[...], heat, preferred_element_type=F32)
+            source = source + bias[:, :1]
             projected[c, :, r] = source.astype(BF16).reshape(DEV, 16, NY)
             return 0
 
@@ -273,11 +374,16 @@
         def group(g, _):
             x0 = g * 16
             load = [halves(joule_ref[z, pl.ds(x0, 16), :]) for z in range(2)]
+            rows = []
             for k in range(16):
                 kept, source = row_of(settled, x0 + k), row_of(returned, x0 + k)
-                for h in range(2):
-                    value = kept[h] + spread(load[0][h], load[1][h], k) * source[h]
-                    out_ref[x0 + k, :, pl.ds(h * LANES, LANES)] = value.astype(BF16)
+                value = [
+                    kept[h] + spread(load[0][h], load[1][h], k) * source[h] for h in range(2)
+                ]
+                rows.append(jnp.concatenate(value, axis=1).astype(BF16))
+            rows = jnp.concatenate(rows, axis=0)
+            block = jnp.dot(swap[...], rows, preferred_element_type=F32).astype(BF16)
+            out_ref[:, :, pl.ds(x0, 16), :] = block.reshape(2, 8, 16, NY)
             return 0
 
         n = E // 16
@@ -302,8 +408,9 @@
 
     for c in range(CHUNKS):
         left, right = halo_copies(c)
-        pl.when(s > 0)(left.wait_send)
-        pl.when(s < SPACE - 1)(right.wait_send)
+        if left is not None:
+            pl.when((s > 0) | by_relay)(left.wait_send)
+            pl.when((s < SPACE - 1) | by_relay)(right.wait_send)
         sent = settled.at[pl.ds(0, (DEV - 1) * R)]
         pltpu.make_async_copy(sent, sent, fwd_send.at[c]).wait()
         pltpu.make_async_copy(sent, sent, back_send.at[c]).wait()
@@ -312,34 +419,18 @@
 def on_device(
     mode_field, diffusion, joule_load, chaos_basis, quad_weight, base_conductivity, thermal_slope
 ):
-    planes, modes = mode_field.shape[:2]
-    points = chaos_basis.shape[0]
-    field = jnp.transpose(mode_field, (2, 0, 1, 3)).reshape(NX, planes * modes, NY)
-
-    level = quad_weight * base_conductivity
-    swing = level * thermal_slope
-    basis = chaos_basis.astype(F32)
-    eye = jnp.eye(planes, dtype=F32)
-    pad = ((0, QP - points), (0, 0))
-    split = jnp.pad(basis, pad).reshape(QP, DEV, modes)
-    w1 = split[None, :, :, None, :] * eye[:, None, None, :, None]
-    w1 = w1.reshape(planes * QP, DEV * planes * modes).astype(BF16)
-    split = jnp.pad(basis * swing[:, None], pad).reshape(QP, DEV, modes)
-    split = jnp.transpose(split, (1, 2, 0))
-    w2 = split[:, None, :, None, :] * eye[None, :, None, :, None]
-    w2 = w2.reshape(DEV * planes * modes, planes * QP).astype(BF16)
-    bias = jnp.sum(basis * level[:, None], axis=0).reshape(DEV, 1, modes, 1)
-    bias = jnp.broadcast_to(bias, (DEV, planes, modes, LANES)).reshape(-1, LANES)
-
     vmem = pl.BlockSpec(memory_space=pltpu.VMEM)
     rows16 = (NX, 16, NY)
     halo = (GROUPS, 17, 16, NY)
-    out = pl.pallas_call(
+    return pl.pallas_call(
         kernel,
-        out_shape=jax.ShapeDtypeStruct(rows16, BF16),
-        in_specs=[vmem] * 6,
+        out_shape=jax.ShapeDtypeStruct(mode_field.shape, BF16),
+        in_specs=[vmem] * 7,
         out_specs=vmem,
         scratch_shapes=[
+            pltpu.VMEM(rows16, BF16),
+            pltpu.VMEM((256, 256), BF16),
+            pltpu.VMEM(halo, BF16),
             pltpu.VMEM(halo, BF16),
             pltpu.VMEM(halo, BF16),
             pltpu.VMEM(halo, BF16),
@@ -350,8 +441,12 @@
             pltpu.VMEM((CHUNKS, DEV, R, 16, NY), BF16),
             pltpu.VMEM((CHUNKS, DEV, R, 16, NY), BF16),
             pltpu.VMEM(rows16, BF16),
+            pltpu.VMEM((2 * QP, 2 * LANES), BF16),
+            pltpu.VMEM((2 * LANES, 2 * QP), BF16),
+            pltpu.VMEM((2 * LANES, LANES), F32),
             pltpu.SemaphoreType.DMA((2, CHUNKS)),
             pltpu.SemaphoreType.DMA((2, CHUNKS)),
+            pltpu.SemaphoreType.DMA((CHUNKS,)),
             pltpu.SemaphoreType.DMA((CHUNKS,)),
             pltpu.SemaphoreType.DMA((CHUNKS,)),
             pltpu.SemaphoreType.DMA((CHUNKS,)),
@@ -363,8 +458,15 @@
         cost_estimate=pl.CostEstimate(
             flops=3 * 10**9, bytes_accessed=6 * 2**20, transcendentals=3 * 10**6
         ),
-    )(field, diffusion, joule_load, w1, w2, bias)
-    return jnp.transpose(out.reshape(NX, planes, modes, NY), (1, 2, 0, 3))
+    )(
+        mode_field,
+        diffusion,
+        joule_load,
+        chaos_basis,
+        quad_weight,
+        base_conductivity,
+        thermal_slope,
+    )
 
 
 def solution(mesh):

time: 127 us -> 96.4 us (0.76)
  Pallas kernels: 115 us -> 93.2 us
  local copies, waits for them, and re-layouts: 10.5 us -> 3.1 us
  other arithmetic: 1.49 us -> 0 us
    pallas_call x1, Pallas kernels: 115 us -> 93.2 us  [on_device(): pl.pallas_call(kernel, out_shape=jax.ShapeDtypeStruct(mode_field.shape, B...]
    reshape x1 -> x0, local copies, waits for them, and re-layouts: 3.63 us -> none  [on_device(): return jnp.transpose(out.reshape(NX, planes, modes, NY), (1, 2, 0, 3))]
    transpose x2 -> x0, local copies, waits for them, and re-layouts: 2.51 us -> none  [the longest x1 2.49 us: on_device(): jnp.transpose(mode_field, (2, 0, 1, 3)).reshape(NX, planes * modes, NY)]
    convert_element_type x4 -> x0, local copies, waits for them, and re-layouts: 2.35 us -> none  [the longest x2 1.2 us: on_device(): w1 = w1.reshape(planes * QP, DEV * planes * modes).astype(BF16)]
    unnamed x3 -> x1, local copies, waits for them, and re-layouts: 1.01 us -> 3.1 us
where the time goes in v2:
time: 96.4 us; the launch traced here: 96.3 us
  Pallas kernels  93.2 us (97%)
  local copies, waits for them, and re-layouts  3.1 us (3%)
    pallas_call x1, Pallas kernels, on_device(): pl.pallas_call(kernel, out_shape=jax.ShapeDtypeStruct(mode_field.shape, B...  93.2 us
    unnamed x1, local copies, waits for them, and re-layouts  3.1 us

profile of v2, /device:TPU:1, one launch (start us, length us, event | category | flops | bytes accessed | tf_op | source)
XLA Modules:
  0.0 96.3 jit_solution(2722753719459851594)
XLA Ops:
  0.0 93.2 %shard_map.73 = bf16[2,8,256,256]{3,2,1,0:T(8,128)(2,1)} custom-call(bf16[2,8,256,256]{3,2,1,0:T(8,128)(2,1)} %field_ref.1, f32[2,256,256]{2,1,0:T(8,128)} %d_ref.1, f32[2,256,256]{2,1,0:T(8,128)} %joule_ref.1, bf16[343,128]{1,0:T(8,128)(2,1)} %basis_ref.1, f32[343]{0:T(512)} %weight_ref.1, f32[343]{0:T(512)} %base_ref.1, f32[343]{0:T(512)} %slope_ref.1), custom_call_target="tpu_custom_call" | custom-call | flops 3000000000 | bytes 6291456 | tf_op jit(solution)/shard_map/pallas_call | solution.py:425
  93.2 3.1 %copy.9 = bf16[2,8,256,256]{3,2,1,0:T(8,128)(2,1)} copy(bf16[2,8,256,256]{3,2,1,0:T(8,128)(2,1)} %shard_map.73) | data formatting | bytes 4194304

commit v3 on v2

--- a/solution.py
+++ b/solution.py
@@ -21,6 +21,7 @@
 CHUNKS = 8
 E = NX // CHUNKS
 R = E // DEV
+PIECES = ((0, 64), (64, 64), (128, 128))
 QP = 352
 
 
@@ -51,8 +52,8 @@
 
 
 def kernel(
-    field_ref, d_ref, joule_ref, basis_ref, weight_ref, base_ref, slope_ref, out_ref,
-    v_ref, swap,
+    field_hbm, d_ref, joule_ref, basis_ref, weight_ref, base_ref, slope_ref, out_ref,
+    field_ref, v_ref, swap, load_sem,
     to_l, to_r, from_l, from_r, relayed, part, first, settled, gathered, projected, returned,
     w1, w2, bias,
     halo_send, halo_recv, relay_recv, fwd_send, fwd_recv, back_send, back_recv,
@@ -60,6 +61,15 @@
     s = lax.axis_index("space")
     m = lax.axis_index("modes")
 
+    def load(i):
+        rows = pl.ds(*PIECES[i])
+        return pltpu.make_async_copy(
+            field_hbm.at[:, :, rows, :], field_ref.at[:, :, rows, :], load_sem.at[i]
+        )
+
+    for i in range(len(PIECES)):
+        load(i).start()
+
     barrier = pltpu.get_barrier_semaphore()
 
     def greet(k, _):
@@ -106,6 +116,7 @@
         rows = jnp.dot(swap[...], block, preferred_element_type=F32)
         v_ref[pl.ds(x0, 16)] = rows.astype(BF16).reshape(16, 16, NY)
 
+    load(0).wait()
     regroup(0)
 
     def sweep_group(g, _):
@@ -247,6 +258,9 @@
 
     for c in range(CHUNKS):
         a, n = span(c)
+        for i, (start, _) in enumerate(PIECES):
+            if a * 16 < start <= (a + n) * 16 or (c == CHUNKS - 1 and start > (a + n) * 16):
+                load(i).wait()
         lax.fori_loop(a, a + n, sweep_group, 0)
         if c == 0:
             ends = jnp.where(is_end, 1, 0)
@@ -422,14 +436,17 @@
     vmem = pl.BlockSpec(memory_space=pltpu.VMEM)
     rows16 = (NX, 16, NY)
     halo = (GROUPS, 17, 16, NY)
+    anywhere = pl.BlockSpec(memory_space=pl.ANY)
     return pl.pallas_call(
         kernel,
-        out_shape=jax.ShapeDtypeStruct(mode_field.shape, BF16),
-        in_specs=[vmem] * 7,
+        out_shape=pltpu.VMEM(mode_field.shape, BF16),
+        in_specs=[anywhere] + [vmem] * 6,
         out_specs=vmem,
         scratch_shapes=[
+            pltpu.VMEM(mode_field.shape, BF16),
             pltpu.VMEM(rows16, BF16),
             pltpu.VMEM((256, 256), BF16),
+            pltpu.SemaphoreType.DMA((len(PIECES),)),
             pltpu.VMEM(halo, BF16),
             pltpu.VMEM(halo, BF16),
             pltpu.VMEM(halo, BF16),

time: 96.4 us -> 92.7 us (0.962)
  Pallas kernels: 93.2 us -> 91.2 us
  local copies, waits for them, and re-layouts: 3.1 us -> 1.32 us
    pallas_call x1, Pallas kernels: 93.2 us -> 91.2 us  [on_device(): pl.pallas_call(kernel, out_shape=pltpu.VMEM(mode_field.shape, BF16), in_s...]
    unnamed x1, local copies, waits for them, and re-layouts: 3.1 us -> 1.32 us
where the time goes in v3:
time: 92.7 us; the launch traced here: 92.5 us
  Pallas kernels  91.2 us (98%)
  local copies, waits for them, and re-layouts  1.32 us (1%)
    pallas_call x1, Pallas kernels, on_device(): pl.pallas_call(kernel, out_shape=pltpu.VMEM(mode_field.shape, BF16), in_s...  91.2 us

profile of v3, /device:TPU:1, one launch (start us, length us, event | category | flops | bytes accessed | tf_op | source)
XLA Modules:
  0.0 92.5 jit_solution(11831605000119036677)
XLA Ops:
  0.0 91.2 %shard_map.73 = bf16[2,8,256,256]{3,2,1,0:T(8,128)(2,1)S(1)} custom-call(bf16[2,8,256,256]{3,2,1,0:T(8,128)(2,1)} %field_hbm.1, f32[2,256,256]{2,1,0:T(8,128)} %d_ref.1, f32[2,256,256]{2,1,0:T(8,128)} %joule_ref.1, bf16[343,128]{1,0:T(8,128)(2,1)} %basis_ref.1, f32[343]{0:T(512)} %weight_ref.1, f32[343]{0:T(512)} %base_ref.1, f32[343]{0:T(512)} %slope_ref.1), custom_call_target="tpu_custom_call" | custom-call | flops 3000000000 | bytes 6291456 | tf_op jit(solution)/shard_map/pallas_call | solution.py:440
  91.2 1.3 %copy.9 = bf16[2,8,256,256]{3,2,1,0:T(8,128)(2,1)} copy(bf16[2,8,256,256]{3,2,1,0:T(8,128)(2,1)S(1)} %shard_map.73) | data formatting | bytes 4194304
